TPU v7x, 128 devices: a whole 4x4x4 slice. The times are simulated.
128 devices in a mesh: tm: 8 (over y, core), expert: 16 (over z, x).
Axes of the slice: x: 4, y: 4, z: 4, core: 2. Of those that a mesh axis runs over, the one named last changes fastest.
Arguments:
- queries: bfloat16 [16384, 2048], P(('tm', 'expert')), may hold values from -6 to 6
- keys: bfloat16 [16384, 2048], P(('tm', 'expert')), may hold values from -6 to 6
- values: bfloat16 [16384, 2048], P(('tm', 'expert')), may hold values from -6 to 6
- out_grad: bfloat16 [16384, 2048], P(('tm', 'expert')), may hold values from -6 to 6
- expert_ids: int32 [16384, 2], P(('tm', 'expert')), may hold values from 0 to 31, all different within a row
- combine_gates: float32 [16384, 2], P(('tm', 'expert')), may hold values from 0.2 to 1
- gate_weight: bfloat16 [128, 2048, 512], P(('tm', 'expert')), may hold values from -0.125 to 0.125
- up_weight: bfloat16 [128, 2048, 512], P(('tm', 'expert')), may hold values from -0.125 to 0.125
- down_weight: bfloat16 [128, 512, 2048], P(('tm', 'expert')), may hold values from -0.125 to 0.125
Outputs:
- query_grad: bfloat16 [16384, 2048], P(('tm', 'expert'))
- key_grad: bfloat16 [16384, 2048], P(('tm', 'expert'))
- value_grad: bfloat16 [16384, 2048], P(('tm', 'expert'))
- gate_weight_grad: float32 [128, 2048, 512], P(('tm', 'expert'))
- up_weight_grad: float32 [128, 2048, 512], P(('tm', 'expert'))
- down_weight_grad: float32 [128, 512, 2048], P(('tm', 'expert'))
Inputs may be any that keep to these rules, and one draw needn't show every extreme that they name: `expert_ids`: the two experts of a token differ.
All inputs are finite; a program needn't handle non-finite values.
Results may differ from a plain program's by a relative error of at most 0.017.
Values may be sent and summed in bfloat16 or wider, within the bound.
A program may use at most 192 MiB of HBM per device.

v0:
```python
import jax
import jax.numpy as jnp
from jax import lax
from jax.sharding import PartitionSpec as P

HEADS = 16
HEAD_DIM = 128
SLICES = 4
epsilon = 1e-06
highest = lax.Precision.HIGHEST


def side_by_side(arrays, axis, split_dim, concat_dim, along):
    widths = [a.shape[along] for a in arrays]
    both = jnp.concatenate(arrays, axis=along)
    whole = lax.all_to_all(both, axis, split_axis=split_dim, concat_axis=concat_dim, tiled=True)
    return tuple(jnp.split(whole, [sum(widths[:k]) for k in range(1, len(widths))], axis=along))


def slot_places(routes, capacity, experts):
    flat_ids = routes.reshape(-1)
    onehot = (flat_ids[:, None] == jnp.arange(experts, dtype=jnp.int32)[None, :]).astype(jnp.int32)
    earlier = jnp.cumsum(onehot, axis=0) - onehot
    position = jnp.sum(earlier * onehot, axis=1)
    return jnp.where(position < capacity, flat_ids * capacity + position, experts * capacity)


def expert_slice(rows, grad_rows, gate_part, up_part, down_part):
    gate = jnp.dot(rows, gate_part, preferred_element_type=jnp.float32)
    upper = jnp.dot(rows, up_part, preferred_element_type=jnp.float32)
    sigma = jax.nn.sigmoid(gate)
    act = (gate * sigma * upper).astype(jnp.bfloat16)
    act_grad = jnp.dot(grad_rows, down_part.T, preferred_element_type=jnp.float32)
    down_grad = jnp.dot(act.T, grad_rows, preferred_element_type=jnp.float32)
    gate_grad = (act_grad * upper * sigma * (1.0 + gate * (1.0 - sigma))).astype(jnp.bfloat16)
    up_grad = (act_grad * gate * sigma).astype(jnp.bfloat16)
    gate_wgrad = jnp.dot(rows.T, gate_grad, preferred_element_type=jnp.float32)
    up_wgrad = jnp.dot(rows.T, up_grad, preferred_element_type=jnp.float32)
    partial_sum = jnp.dot(gate_grad, gate_part.T, preferred_element_type=jnp.float32)
    partial_sum = partial_sum + jnp.dot(up_grad, up_part.T, preferred_element_type=jnp.float32)
    return (partial_sum.astype(jnp.bfloat16), gate_wgrad, up_wgrad, down_grad)


def body(
    queries, keys, values, out_grad, expert_ids, combine_gates, gate_weight, up_weight, down_weight
):
    tok_rows = queries.shape[0]
    width = queries.shape[1]
    time_count = lax.axis_size("tm")
    group_count = lax.axis_size("expert")
    devices = time_count * group_count
    experts = devices // SLICES
    capacity = SLICES * max(1, 3 * tok_rows // (experts * SLICES))
    shape3 = (tok_rows, HEADS, HEAD_DIM)
    query_f = queries.astype(jnp.float32).reshape(shape3)
    key_f = keys.astype(jnp.float32).reshape(shape3)
    value_f = values.astype(jnp.float32).reshape(shape3)
    local = jnp.einsum("tha,thb->hab", key_f, value_f, precision=highest)
    everyone = lax.all_gather(local[None], "tm", axis=0, tiled=True)
    mine = lax.axis_index("tm")
    picks = (jnp.arange(everyone.shape[0], dtype=jnp.int32) <= mine).astype(jnp.float32)
    inclusive = jnp.einsum("c,chab->hab", picks, everyone, precision=highest)
    states = lax.psum(inclusive, "expert")
    mixed = jnp.einsum("tha,hab->thb", query_f, states, precision=highest)
    scale = lax.rsqrt(jnp.mean(mixed * mixed, axis=-1, keepdims=True) + epsilon)
    normed = mixed * scale
    hidden = normed.astype(jnp.bfloat16).reshape(tok_rows, width)
    places = slot_places(expert_ids, capacity, experts)
    rows_h = jnp.repeat(hidden, 2, axis=0)
    grad_f = out_grad.astype(jnp.float32)
    rows_g = (jnp.repeat(grad_f, 2, axis=0) * combine_gates.reshape(-1, 1)).astype(jnp.bfloat16)
    buffer_h = (
        jnp.zeros((experts * capacity, width), jnp.bfloat16).at[places].set(rows_h, mode="drop")
    )
    buffer_g = (
        jnp.zeros((experts * capacity, width), jnp.bfloat16).at[places].set(rows_g, mode="drop")
    )
    send_h = jnp.repeat(buffer_h.reshape(experts, capacity, width), SLICES, axis=0)
    send_g = jnp.repeat(buffer_g.reshape(experts, capacity, width), SLICES, axis=0)
    got_h, got_g = side_by_side((send_h, send_g), ("tm", "expert"), 0, 0, 1)
    got_h = got_h.reshape(1, devices, capacity, width)
    got_g = got_g.reshape(1, devices, capacity, width)
    rows = got_h.reshape(-1, width)
    grad_rows = got_g.reshape(-1, width)
    partial_sum, gate_wgrad, up_wgrad, down_grad = expert_slice(
        rows, grad_rows, gate_weight[0], up_weight[0], down_weight[0]
    )
    payload = partial_sum.astype(jnp.float32).reshape(devices, capacity, width)
    returned = lax.all_to_all(
        payload.astype(jnp.bfloat16), ("tm", "expert"), split_axis=0, concat_axis=0, tiled=True
    ).astype(payload.dtype)
    summed = jnp.sum(returned.reshape(experts, SLICES, capacity, width), axis=1)
    per_choice = jnp.take(
        summed.reshape(experts * capacity, width), places, axis=0, mode="fill", fill_value=0.0
    )
    moe_grad = jnp.sum(per_choice.reshape(tok_rows, 2, width), axis=1)
    hidden_grad = (grad_f + moe_grad).reshape(shape3)
    norm_grad = scale * (
        hidden_grad - normed * jnp.mean(hidden_grad * normed, axis=-1, keepdims=True)
    )
    query_grad = jnp.einsum("thb,hab->tha", norm_grad, states, precision=highest)
    local_back = jnp.einsum("tha,thb->hab", query_f, norm_grad, precision=highest)
    every_back = lax.all_gather(
        local_back[None].astype(jnp.bfloat16), "tm", axis=0, tiled=True
    ).astype(jnp.float32)
    mine_back = lax.axis_index("tm")
    picks_back = (jnp.arange(every_back.shape[0], dtype=jnp.int32) >= mine_back).astype(jnp.float32)
    inclusive_back = jnp.einsum("c,chab->hab", picks_back, every_back, precision=highest)
    back_states = lax.psum(inclusive_back.astype(jnp.bfloat16), "expert").astype(jnp.float32)
    key_grad = jnp.einsum("thb,hab->tha", value_f, back_states, precision=highest)
    value_grad = jnp.einsum("tha,hab->thb", key_f, back_states, precision=highest)
    return (
        query_grad.reshape(tok_rows, width).astype(jnp.bfloat16),
        key_grad.reshape(tok_rows, width).astype(jnp.bfloat16),
        value_grad.reshape(tok_rows, width).astype(jnp.bfloat16),
        gate_wgrad[None],
        up_wgrad[None],
        down_grad[None],
    )


def solution(mesh):
    placed = (
        P(("tm", "expert"), None),
        P(("tm", "expert"), None),
        P(("tm", "expert"), None),
        P(("tm", "expert"), None),
        P(("tm", "expert"), None),
        P(("tm", "expert"), None),
        P(("tm", "expert"), None, None),
        P(("tm", "expert"), None, None),
        P(("tm", "expert"), None, None),
    )
    return jax.shard_map(
        body,
        mesh=mesh,
        in_specs=placed,
        out_specs=(
            P(("tm", "expert"), None),
            P(("tm", "expert"), None),
            P(("tm", "expert"), None),
            P(("tm", "expert"), None, None),
            P(("tm", "expert"), None, None),
            P(("tm", "expert"), None, None),
        ),
        check_vma=False,
    )
```

profile of v0, /device:TPU:0, one launch (start us, length us, event | category | flops | bytes accessed | tf_op | source)
XLA Modules:
  0.0 693.4 jit_solution(2359564202389222377)
XLA Ops:
  7.2 2.7 fusion.23
  10.0 52.6 %all-gather.5.cloned.1.call-done = f32[128,128,128]{2,1,0:T(8,128)} async-done(((f32[16,128,128]{2,1,0:T(8,128)}), f32[128,128,128]{2,1,0:T(8,128)}) %all-gather.5.cloned.1.call-update) | async-done | bytes 8388624 | tf_op jit(solution)/shard_map/all_gather | solution.py:59
  62.5 11.8 %fusion = f32[1,16,128,128]{3,0,2,1:T(1,128)S(1)} fusion(f32[8,16,128,128]{3,2,1,0:T(8,128)} %bitcast.136, s32[]{:T(128)S(6)} %axis_index.19), kind=kOutput, calls=%fused_computation.6 | convolution fusion | flops 25165832 | bytes 9437188 | tf_op jit(solution)/shard_map/c,chab->hab/dot_general | solution.py:62
  74.4 2.1 copy.71
  76.5 0.1 copy.52
  76.7 0.1 eq.29
  76.8 0.1 eq.25
  77.0 0.6 reduce-window.6
  77.5 0.2 slice_reduce_fusion
  77.8 0.1 mul.85
  77.9 0.1 copy.57
  78.1 0.1 mul.87
  78.2 3.4 broadcast_in_dim.52
  81.6 3.6 reshape.151
  85.4 4.5 scatter_custom_fusion.1
  89.9 3.6 reshape.152
  93.5 70.4 %all-reduce.3.cloned.1.call-done = f32[16,128,128]{1,2,0:T(8,128)} async-done(((f32[16,128,128]{1,2,0:T(8,128)}), f32[16,128,128]{1,2,0:T(8,128)}) %all-reduce.3.cloned.1.call-update) | async-done | bytes 1048592 | tf_op jit(solution)/shard_map/psum | solution.py:63
  164.0 2.4 multiply_reduce_fusion.1
  166.4 1.0 copy-done.2
  167.4 0.1 multiply_convert_fusion.6
  167.5 1.0 copy.56
  168.6 1.7 broadcast_in_dim.50
  170.2 1.2 reshape.172
  171.5 4.1 scatter_custom_fusion
  175.6 3.6 reshape.149
  179.2 6.1 broadcast_in_dim.53
  185.2 4.3 broadcast_in_dim.51
  189.5 9.2 %pad_maximum_fusion = bf16[128,24,2048]{2,1,0:T(8,128)(2,1)S(1)} fusion(bf16[128,12,2048]{2,1,0:T(8,128)(2,1)} %bitcast.132, bf16[128,12,2048]{2,1,0:T(8,128)(2,1)} %bitcast.133), kind=kLoop, calls=%fused_computation.4 | loop fusion | flops 25165824 | bytes 25165824 | tf_op jit(solution)/shard_map/concatenate | solution.py:15
  198.7 149.2 %all_to_all.10 = bf16[128,24,2048]{2,1,0:T(8,128)(2,1)S(1)} all-to-all(bf16[128,24,2048]{2,1,0:T(8,128)(2,1)S(1)} %pad_maximum_fusion), channel_id=1, replica_groups=mesh['tm'=8,'expert'=16] {'tm','expert'}, dimensions={0} | all-to-all | bytes 25165824 | tf_op jit(solution)/shard_map/all_to_all | solution.py:16
  347.9 7.1 %fusion.46 = (bf16[128,12,2048]{2,1,0:T(8,128)(2,1)}, bf16[128,12,2048]{2,1,0:T(8,128)(2,1)}) fusion(bf16[128,24,2048]{2,1,0:T(8,128)(2,1)S(1)} %all_to_all.10), kind=kLoop, calls=%fused_computation.84 | loop fusion | bytes 25165824 | tf_op jit(solution)/shard_map/split | solution.py:17
  355.0 10.7 %reshape_reshape.6 = bf16[1536,2048]{1,0:T(8,128)(2,1)} reshape(bf16[128,12,2048]{2,1,0:T(8,128)(2,1)} %get-tuple-element.24) | data formatting | bytes 12582912 | tf_op jit(solution)/shard_map/reshape;reshape | solution.py:84
  365.7 10.7 %reshape_reshape.7 = bf16[1536,2048]{1,0:T(8,128)(2,1)} reshape(bf16[128,12,2048]{2,1,0:T(8,128)(2,1)} %get-tuple-element.25) | data formatting | bytes 12582912 | tf_op jit(solution)/shard_map/reshape;reshape | solution.py:83
  376.4 6.0 fusion.6
  382.4 3.4 fusion.9
  385.9 4.8 multiply_convert_fusion.1
  390.8 6.5 fusion.4
  397.3 8.5 %add_convert_fusion = bf16[1536,2048]{1,0:T(8,128)(2,1)} fusion(f32[1536,2048]{1,0:T(8,128)} %fusion.4, bf16[1536,512]{1,0:T(8,128)(2,1)S(1)} %get-tuple-element.26, bf16[1,2048,512]{2,1,0:T(8,128)(2,1)S(1)} %copy-done.13), kind=kOutput, calls=%fused_computation.5 | convolution fusion | flops 3227516928 | bytes 22544384 | tf_op jit(solution)/shard_map/dot_general | solution.py:40
  405.8 10.6 %convert_element_type.88 = bf16[128,12,2048]{2,1,0:T(8,128)(2,1)} reshape(bf16[1536,2048]{1,0:T(8,128)(2,1)} %add_convert_fusion) | data formatting | bytes 12582912 | tf_op jit(solution)/shard_map/convert_element_type | solution.py:90
  416.4 6.9 all-to-all-start.1
  423.4 0.1 reduce_sum.51
  423.6 99.8 %all-to-all-done.1 = bf16[128,12,2048]{2,1,0:T(8,128)(2,1)} async-done(((bf16[128,12,2048]{2,1,0:T(8,128)(2,1)}), bf16[128,12,2048]{2,1,0:T(8,128)(2,1)}, u32[]{:S(2)}, u32[]{:S(2)}) %all-to-all-start.1) | async-done | bytes 6291488 | tf_op jit(solution)/shard_map/all_to_all | solution.py:89
  523.4 7.8 %convert_reduce_fusion = f32[32,12,2048]{2,1,0:T(8,128)} fusion(bf16[128,12,2048]{2,1,0:T(8,128)(2,1)} %all-to-all-done.1), kind=kLoop, calls=%fused_computation.3 | loop fusion | flops 5505024 | bytes 9437184 | tf_op jit(solution)/shard_map/reduce_sum | solution.py:92
  531.2 3.0 reshape.156
  534.2 2.7 gather_fusion
  536.9 2.5 gather.7
  539.4 4.5 select_reduce_fusion
  544.0 0.3 copy.58
  544.4 0.8 copy-done.3
  545.1 0.2 multiply_reduce_fusion
  545.3 1.8 fusion.14
  547.1 1.0 copy.62
  548.2 8.9 %convolution_bitcast_fusion.1 = f32[1,2048,512]{2,1,0:T(8,128)} fusion(bf16[1536,2048]{1,0:T(8,128)(2,1)} %reshape_reshape.7, bf16[1536,512]{1,0:T(8,128)(2,1)} %copy-done.14), kind=kOutput, calls=%fused_computation.11 | convolution fusion | flops 3221225472 | bytes 12058624 | tf_op jit(solution)/shard_map/dot_general | solution.py:38
  557.1 8.3 %convolution_bitcast_fusion = f32[1,512,2048]{2,1,0:T(8,128)} fusion(bf16[1536,2048]{1,0:T(8,128)(2,1)} %reshape_reshape.6, f32[1536,512]{1,0:T(8,128)S(1)} %copy-done.19, f32[1536,512]{1,0:T(8,128)S(1)} %copy-done.17), kind=kOutput, calls=%fused_computation.10 | convolution fusion | flops 3225944064 | bytes 16777216 | tf_op jit(solution)/shard_map/dot_general | solution.py:34
  565.4 24.5 %all-gather.7.cloned.1.call-done = bf16[128,128,128]{2,1,0:T(8,128)(2,1)} async-done(((bf16[16,128,128]{2,1,0:T(8,128)(2,1)}), bf16[128,128,128]{2,1,0:T(8,128)(2,1)}) %all-gather.7.cloned.1.call-update) | async-done | bytes 4194320 | tf_op jit(solution)/shard_map/all_gather | solution.py:103
  589.9 4.9 fusion.2
  594.9 0.9 convert_element_type.95
  595.8 8.8 %convolution_bitcast_fusion.2 = f32[1,2048,512]{2,1,0:T(8,128)} fusion(bf16[1536,2048]{1,0:T(8,128)(2,1)} %reshape_reshape.7, bf16[1536,512]{1,0:T(8,128)(2,1)} %copy-done.15), kind=kOutput, calls=%fused_computation.12 | convolution fusion | flops 3221225472 | bytes 12058624 | tf_op jit(solution)/shard_map/dot_general | solution.py:37
  604.6 2.0 convolution_convert_fusion.3
  606.6 1.0 copy.66
  607.6 73.6 %all-reduce.5.cloned.1.call-done = bf16[16,128,128]{2,1,0:T(8,128)(2,1)} async-done(((bf16[16,128,128]{2,1,0:T(8,128)(2,1)}), bf16[16,128,128]{2,1,0:T(8,128)(2,1)}) %all-reduce.5.cloned.1.call-update) | async-done | bytes 524304 | tf_op jit(solution)/shard_map/psum | solution.py:109
  681.2 1.5 convolution_convert_fusion.1
  682.7 1.0 copy.67
  683.7 1.7 convolution_convert_fusion
  685.4 1.0 copy.68
  (62 shorter events, 0.7 us)
Async XLA Ops:
  7.2 369.2 %copy-start = (bf16[1,2048,512]{2,1,0:T(8,128)(2,1)S(1)}, bf16[1,2048,512]{2,1,0:T(8,128)(2,1)}, u32[]{:S(2)}) copy-start(bf16[1,2048,512]{2,1,0:T(8,128)(2,1)} %param.15) | copy-start | bytes 6291460
  7.2 55.4 %all-gather.5.cloned.1.call-start = ((), (), s32[]{:S(2)}) async-start(), calls=%async_computation.4 | async-start | bytes 9437184 | tf_op jit(solution)/shard_map/all_gather | solution.py:59
  9.9 154.0 %all-reduce.3.cloned.1.call-start = ((), (), s32[]{:S(2)}) async-start(), calls=%async_computation.2 | async-start | bytes 2097152 | tf_op jit(solution)/shard_map/psum | solution.py:63
  74.4 2.1 copy-start.10
  74.4 3.5 copy-start.11
  85.4 78.6 %copy-start.8 = (bf16[128,2048]{1,0:T(8,128)(2,1)S(1)}, bf16[128,2048]{1,0:T(8,128)(2,1)}, u32[]{:S(2)}) copy-start(bf16[128,2048]{1,0:T(8,128)(2,1)} %param.9) | copy-start | bytes 1572868
  166.4 1.0 copy-start.2
  179.2 6.1 copy-start.4
  376.4 6.0 copy-start.5
  376.4 6.0 copy-start.13
  376.4 9.5 %slice-start = ((s8[6291456]{0:T(1024)(128)(4,1)}), s8[4194304]{0:T(1024)(128)(4,1)S(1)}, s32[]{:S(2)}) async-start(s8[6291456]{0:T(1024)(128)(4,1)} %bitcast.137), calls=%async_computation.6 | async-start | bytes 8388608
  382.4 3.5 copy-start.16
  382.4 3.5 slice-start.1
  382.4 3.5 copy-start.12
  385.9 4.9 copy-start.18
  390.8 6.5 copy-start.15
  390.8 6.5 copy-start.14
  416.4 106.9 %all-to-all-start.1 = ((bf16[128,12,2048]{2,1,0:T(8,128)(2,1)}), bf16[128,12,2048]{2,1,0:T(8,128)(2,1)}, u32[]{:S(2)}, u32[]{:S(2)}) async-start(bf16[128,12,2048]{2,1,0:T(8,128)(2,1)} %convert_element_type.88), calls=%async_computation.1 | async-start | bytes 16777216 | tf_op jit(solution)/shard_map/all_to_all | solution.py:89
  423.3 166.6 %all-gather.7.cloned.1.call-start = ((), (), s32[]{:S(2)}) async-start(), calls=%async_computation.5 | async-start | bytes 4718592 | tf_op jit(solution)/shard_map/all_gather | solution.py:103
  539.4 4.5 copy-start.7
  543.9 1.2 copy-start.3
  548.2 133.0 %all-reduce.5.cloned.1.call-start = ((), (), s32[]{:S(2)}) async-start(), calls=%async_computation.3 | async-start | bytes 1048576 | tf_op jit(solution)/shard_map/psum | solution.py:109
  548.2 8.9 %copy-start.17 = (f32[1536,512]{1,0:T(8,128)S(1)}, f32[1536,512]{1,0:T(8,128)}, u32[]{:S(2)}) copy-start(f32[1536,512]{1,0:T(8,128)} %copy-done.16) | copy-start | bytes 9437188
  548.2 8.9 %copy-start.19 = (f32[1536,512]{1,0:T(8,128)S(1)}, f32[1536,512]{1,0:T(8,128)}, u32[]{:S(2)}) copy-start(f32[1536,512]{1,0:T(8,128)} %copy-done.18) | copy-start | bytes 9437188
  595.8 8.8 %copy-start.6 = (f32[16,128,128]{1,2,0:T(8,128)S(1)}, f32[16,128,128]{1,2,0:T(8,128)}, u32[]{:S(2)}) copy-start(f32[16,128,128]{1,2,0:T(8,128)} %all-reduce.3.cloned.1.call-done) | copy-start | bytes 3145732
  604.6 76.6 %copy-start.9 = (bf16[128,2048]{1,0:T(8,128)(2,1)S(1)}, bf16[128,2048]{1,0:T(8,128)(2,1)}, u32[]{:S(2)}) copy-start(bf16[128,2048]{1,0:T(8,128)(2,1)} %param.11) | copy-start | bytes 1572868
  606.6 79.9 %copy-start.1 = (bf16[1,2048,512]{2,1,0:T(8,128)(2,1)S(1)}, bf16[1,2048,512]{2,1,0:T(8,128)(2,1)}, u32[]{:S(2)}) copy-start(bf16[1,2048,512]{2,1,0:T(8,128)(2,1)} %param.15) | copy-start | bytes 6291460
Sparse Core Ops, SparseCore 0:
  10.3 52.1 all-gather.4
  76.7 87.2 all-reduce.2
  548.3 41.5 all-gather.6
  595.9 85.2 all-reduce.4
where the time goes:
time: 702 us; the launch traced here: 693 us
  waiting for transfers between devices  321 us (46%)
  blocking collectives  149 us (21%)
  local copies, waits for them, and re-layouts  89.3 us (13%)
  matrix products  84.1 us (12%)
  other arithmetic  28.2 us (4%)
  between operations  14.6 us (2%)
    all_to_all x1, blocking collectives, side_by_side(): lax.all_to_all(both, axis, split_axis=split_dim, concat_axis=concat_dim,...  149 us
    all_to_all x1, waiting for transfers between devices, body(): lax.all_to_all(payload.astype(jnp.bfloat16), ('tm', 'expert'), split_axis...  99.8 us
    psum x1, waiting for transfers between devices, body(): lax.psum(inclusive_back.astype(jnp.bfloat16), 'expert').astype(jnp.float32)  73.6 us
    psum x1, waiting for transfers between devices, body(): states = lax.psum(inclusive, 'expert')  70.4 us
    all_gather x1, waiting for transfers between devices, body(): everyone = lax.all_gather(local[None], 'tm', axis=0, tiled=True)  52.6 us
    all_gather x1, waiting for transfers between devices, body(): lax.all_gather(local_back[None].astype(jnp.bfloat16), 'tm', axis=0, tiled...  24.5 us
  transfers between devices with their start and end apart: 5, of which 5 were waited for; matrix products, arithmetic and copies ran while one was open for 7% of the time, Pallas kernels for 0%

commit v1 on v0

--- a/solution.py
+++ b/solution.py
@@ -60,7 +60,7 @@
     mine = lax.axis_index("tm")
     picks = (jnp.arange(everyone.shape[0], dtype=jnp.int32) <= mine).astype(jnp.float32)
     inclusive = jnp.einsum("c,chab->hab", picks, everyone, precision=highest)
-    states = lax.psum(inclusive, "expert")
+    states = jnp.sum(lax.all_gather(inclusive, "expert"), axis=0)
     mixed = jnp.einsum("tha,hab->thb", query_f, states, precision=highest)
     scale = lax.rsqrt(jnp.mean(mixed * mixed, axis=-1, keepdims=True) + epsilon)
     normed = mixed * scale

time: 702 us -> 737 us (1.050)
  waiting for transfers between devices: 321 us -> 347 us
  other arithmetic: 28.2 us -> 36.8 us
    all_gather x0 -> x1, waiting for transfers between devices: none -> 95.5 us  [body(): states = jnp.sum(lax.all_gather(inclusive, 'expert'), axis=0)]
    psum x1 -> x0, waiting for transfers between devices: 70.4 us -> none  [body(): states = lax.psum(inclusive, 'expert')]
    reduce_sum x0 -> x1, other arithmetic: none -> 7.44 us  [body(): states = jnp.sum(lax.all_gather(inclusive, 'expert'), axis=0)]
  transfers between devices with their start and end apart: 5 -> 5, of which waited for: 5 -> 5; matrix products, arithmetic and copies ran while one was open for 7% -> 6% of each run, Pallas kernels for 0% -> 0%
where the time goes in v1:
time: 737 us; the launch traced here: 728 us
  waiting for transfers between devices  347 us (47%)
  blocking collectives  150 us (20%)
  local copies, waits for them, and re-layouts  89.3 us (12%)
  matrix products  84.4 us (11%)
  other arithmetic  36.8 us (5%)
  between operations  14.5 us (2%)
    all_to_all x1, blocking collectives, side_by_side(): lax.all_to_all(both, axis, split_axis=split_dim, concat_axis=concat_dim,...  150 us
    all_to_all x1, waiting for transfers between devices, body(): lax.all_to_all(payload.astype(jnp.bfloat16), ('tm', 'expert'), split_axis...  99.8 us
    all_gather x1, waiting for transfers between devices, body(): states = jnp.sum(lax.all_gather(inclusive, 'expert'), axis=0)  95.5 us
    psum x1, waiting for transfers between devices, body(): lax.psum(inclusive_back.astype(jnp.bfloat16), 'expert').astype(jnp.float32)  74.3 us
    all_gather x1, waiting for transfers between devices, body(): everyone = lax.all_gather(local[None], 'tm', axis=0, tiled=True)  52.6 us
    all_gather x1, waiting for transfers between devices, body(): lax.all_gather(local_back[None].astype(jnp.bfloat16), 'tm', axis=0, tiled...  24.5 us
  transfers between devices with their start and end apart: 5, of which 5 were waited for; matrix products, arithmetic and copies ran while one was open for 6% of the time, Pallas kernels for 0%

profile of v1, /device:TPU:0, one launch (start us, length us, event | category | flops | bytes accessed | tf_op | source)
XLA Modules:
  0.0 728.4 jit_solution(14644235988845267982)
XLA Ops:
  7.2 2.7 fusion.23
  10.0 52.6 %all-gather.7.cloned.1.call-done = f32[128,128,128]{2,1,0:T(8,128)} async-done(((f32[16,128,128]{2,1,0:T(8,128)}), f32[128,128,128]{2,1,0:T(8,128)}) %all-gather.7.cloned.1.call-update) | async-done | bytes 8388624 | tf_op jit(solution)/shard_map/all_gather | solution.py:59
  62.5 12.9 %fusion = f32[1,16,128,128]{3,0,2,1:T(1,128)} fusion(f32[8,16,128,128]{3,2,1,0:T(8,128)} %bitcast.139, s32[]{:T(128)S(6)} %axis_index.19), kind=kOutput, calls=%fused_computation.6 | convolution fusion | flops 25165832 | bytes 9437188 | tf_op jit(solution)/shard_map/c,chab->hab/dot_general | solution.py:62
  75.5 0.1 copy.53
  75.6 0.1 eq.29
  75.7 0.1 eq.25
  75.9 0.8 reduce-window.6
  76.7 0.2 slice_reduce_fusion
  76.9 0.1 mul.85
  77.1 0.1 copy.58
  77.2 0.1 mul.87
  77.3 2.4 broadcast_in_dim.52
  79.7 3.6 reshape.151
  83.5 4.7 scatter_custom_fusion.1
  88.1 3.6 reshape.152
  91.7 95.5 %all-gather.9.cloned.1.call-done = f32[256,128,128]{2,1,0:T(8,128)} async-done(((f32[16,128,128]{2,1,0:T(8,128)}), f32[256,128,128]{2,1,0:T(8,128)}) %all-gather.9.cloned.1.call-update) | async-done | bytes 16777232 | tf_op jit(solution)/shard_map/all_gather | solution.py:63
  187.2 7.4 %reduce_sum.58 = f32[16,128,128]{2,1,0:T(8,128)S(1)} reduce(f32[16,16,128,128]{3,2,1,0:T(8,128)} %bitcast.136, f32[]{:T(128)} %constant.16.clone.1), dimensions={0}, to_apply=%region_0.0 | reduce | flops 3932160 | bytes 17825796 | tf_op jit(solution)/shard_map/reduce_sum | solution.py:63
  194.7 2.4 multiply_reduce_fusion.1
  197.2 1.0 copy-done.2
  198.2 0.9 multiply_convert_fusion.6
  199.1 2.0 copy.57
  201.1 2.6 broadcast_in_dim.50
  203.8 2.2 reshape.172
  206.0 4.1 scatter_custom_fusion
  210.1 3.6 reshape.149
  213.7 6.1 broadcast_in_dim.53
  219.8 4.3 broadcast_in_dim.51
  224.1 9.2 %pad_maximum_fusion = bf16[128,24,2048]{2,1,0:T(8,128)(2,1)S(1)} fusion(bf16[128,12,2048]{2,1,0:T(8,128)(2,1)} %bitcast.134, bf16[128,12,2048]{2,1,0:T(8,128)(2,1)} %bitcast.135), kind=kLoop, calls=%fused_computation.4 | loop fusion | flops 25165824 | bytes 25165824 | tf_op jit(solution)/shard_map/concatenate | solution.py:15
  233.3 149.6 %all_to_all.10 = bf16[128,24,2048]{2,1,0:T(8,128)(2,1)S(1)} all-to-all(bf16[128,24,2048]{2,1,0:T(8,128)(2,1)S(1)} %pad_maximum_fusion), channel_id=1, replica_groups=mesh['tm'=8,'expert'=16] {'tm','expert'}, dimensions={0} | all-to-all | bytes 25165824 | tf_op jit(solution)/shard_map/all_to_all | solution.py:16
  382.9 7.1 fusion.46
  390.0 10.7 %reshape_reshape.6 = bf16[1536,2048]{1,0:T(8,128)(2,1)} reshape(bf16[128,12,2048]{2,1,0:T(8,128)(2,1)} %get-tuple-element.24) | data formatting | bytes 12582912 | tf_op jit(solution)/shard_map/reshape;reshape | solution.py:84
  400.7 10.7 %reshape_reshape.7 = bf16[1536,2048]{1,0:T(8,128)(2,1)} reshape(bf16[128,12,2048]{2,1,0:T(8,128)(2,1)} %get-tuple-element.25) | data formatting | bytes 12582912 | tf_op jit(solution)/shard_map/reshape;reshape | solution.py:83
  411.4 6.0 fusion.6
  417.4 3.4 fusion.9
  420.9 4.8 multiply_convert_fusion.1
  425.8 6.5 fusion.4
  432.3 8.5 %add_convert_fusion = bf16[1536,2048]{1,0:T(8,128)(2,1)} fusion(f32[1536,2048]{1,0:T(8,128)} %fusion.4, bf16[1536,512]{1,0:T(8,128)(2,1)S(1)} %get-tuple-element.26, bf16[1,2048,512]{2,1,0:T(8,128)(2,1)S(1)} %copy-done.14), kind=kOutput, calls=%fused_computation.5 | convolution fusion | flops 3227516928 | bytes 22544384 | tf_op jit(solution)/shard_map/dot_general | solution.py:40
  440.8 10.6 %convert_element_type.88 = bf16[128,12,2048]{2,1,0:T(8,128)(2,1)} reshape(bf16[1536,2048]{1,0:T(8,128)(2,1)} %add_convert_fusion) | data formatting | bytes 12582912 | tf_op jit(solution)/shard_map/convert_element_type | solution.py:90
  451.4 6.9 all-to-all-start.1
  458.3 0.1 reduce_sum.61
  458.5 99.8 %all-to-all-done.1 = bf16[128,12,2048]{2,1,0:T(8,128)(2,1)} async-done(((bf16[128,12,2048]{2,1,0:T(8,128)(2,1)}), bf16[128,12,2048]{2,1,0:T(8,128)(2,1)}, u32[]{:S(2)}, u32[]{:S(2)}) %all-to-all-start.1) | async-done | bytes 6291488 | tf_op jit(solution)/shard_map/all_to_all | solution.py:89
  558.4 7.8 %convert_reduce_fusion = f32[32,12,2048]{2,1,0:T(8,128)} fusion(bf16[128,12,2048]{2,1,0:T(8,128)(2,1)} %all-to-all-done.1), kind=kLoop, calls=%fused_computation.3 | loop fusion | flops 5505024 | bytes 9437184 | tf_op jit(solution)/shard_map/reduce_sum | solution.py:92
  566.2 3.0 reshape.156
  569.2 2.7 gather_fusion
  571.9 2.5 gather.7
  574.4 4.5 select_reduce_fusion
  579.0 0.3 copy.59
  579.4 0.8 copy-done.3
  580.1 0.2 multiply_reduce_fusion
  580.3 1.8 fusion.14
  582.1 1.0 copy.62
  583.2 8.9 %convolution_bitcast_fusion.1 = f32[1,2048,512]{2,1,0:T(8,128)} fusion(bf16[1536,2048]{1,0:T(8,128)(2,1)} %reshape_reshape.7, bf16[1536,512]{1,0:T(8,128)(2,1)} %copy-done.15), kind=kOutput, calls=%fused_computation.11 | convolution fusion | flops 3221225472 | bytes 12058624 | tf_op jit(solution)/shard_map/dot_general | solution.py:38
  592.1 8.3 %convolution_bitcast_fusion = f32[1,512,2048]{2,1,0:T(8,128)} fusion(bf16[1536,2048]{1,0:T(8,128)(2,1)} %reshape_reshape.6, f32[1536,512]{1,0:T(8,128)S(1)} %copy-done.20, f32[1536,512]{1,0:T(8,128)S(1)} %copy-done.18), kind=kOutput, calls=%fused_computation.10 | convolution fusion | flops 3225944064 | bytes 16777216 | tf_op jit(solution)/shard_map/dot_general | solution.py:34
  600.4 24.5 %all-gather.11.cloned.1.call-done = bf16[128,128,128]{2,1,0:T(8,128)(2,1)} async-done(((bf16[16,128,128]{2,1,0:T(8,128)(2,1)}), bf16[128,128,128]{2,1,0:T(8,128)(2,1)}) %all-gather.11.cloned.1.call-update) | async-done | bytes 4194320 | tf_op jit(solution)/shard_map/all_gather | solution.py:103
  624.9 4.9 fusion.2
  629.8 0.9 convert_element_type.95
  630.8 8.8 %convolution_bitcast_fusion.2 = f32[1,2048,512]{2,1,0:T(8,128)} fusion(bf16[1536,2048]{1,0:T(8,128)(2,1)} %reshape_reshape.7, bf16[1536,512]{1,0:T(8,128)(2,1)} %copy-done.16), kind=kOutput, calls=%fused_computation.12 | convolution fusion | flops 3221225472 | bytes 12058624 | tf_op jit(solution)/shard_map/dot_general | solution.py:37
  639.6 1.3 convolution_convert_fusion.3
  640.8 1.0 copy.66
  641.8 74.3 %all-reduce.2.cloned.1.call-done = bf16[16,128,128]{2,1,0:T(8,128)(2,1)} async-done(((bf16[16,128,128]{2,1,0:T(8,128)(2,1)}), bf16[16,128,128]{2,1,0:T(8,128)(2,1)}) %all-reduce.2.cloned.1.call-update) | async-done | bytes 524304 | tf_op jit(solution)/shard_map/psum | solution.py:109
  716.2 1.5 convolution_convert_fusion.1
  717.7 1.0 copy.67
  718.7 1.7 convolution_convert_fusion
  720.4 1.0 copy.68
  (64 shorter events, 0.7 us)
Async XLA Ops:
  7.2 404.2 %copy-start = (bf16[1,2048,512]{2,1,0:T(8,128)(2,1)S(1)}, bf16[1,2048,512]{2,1,0:T(8,128)(2,1)}, u32[]{:S(2)}) copy-start(bf16[1,2048,512]{2,1,0:T(8,128)(2,1)} %param.15) | copy-start | bytes 6291460
  7.2 55.4 %all-gather.7.cloned.1.call-start = ((), (), s32[]{:S(2)}) async-start(), calls=%async_computation.3 | async-start | bytes 9437184 | tf_op jit(solution)/shard_map/all_gather | solution.py:59
  9.9 177.3 %all-gather.9.cloned.1.call-start = ((), (), s32[]{:S(2)}) async-start(), calls=%async_computation.4 | async-start | bytes 17825792 | tf_op jit(solution)/shard_map/all_gather | solution.py:63
  62.5 12.9 %copy-start.11 = (s32[128,2]{0,1:T(2,128)S(1)}, s32[128,2]{0,1:T(2,128)}, u32[]{:S(2)}) copy-start(s32[128,2]{0,1:T(2,128)} %param.13) | copy-start | bytes 3076
  62.5 14.5 %copy-start.12 = (f32[128,2]{0,1:T(2,128)S(1)}, f32[128,2]{0,1:T(2,128)}, u32[]{:S(2)}) copy-start(f32[128,2]{0,1:T(2,128)} %param.14) | copy-start | bytes 3076
  62.5 14.8 %copy-start.8 = (bf16[128,2048]{1,0:T(8,128)(2,1)S(1)}, bf16[128,2048]{1,0:T(8,128)(2,1)}, u32[]{:S(2)}) copy-start(bf16[128,2048]{1,0:T(8,128)(2,1)} %param.12) | copy-start | bytes 1572868
  194.7 9.1 %copy-start.4 = (f32[16,128,128]{2,1,0:T(8,128)}, f32[16,128,128]{2,1,0:T(8,128)S(1)}, u32[]{:S(2)}) copy-start(f32[16,128,128]{2,1,0:T(8,128)S(1)} %reduce_sum.58) | copy-start | bytes 3145732
  197.1 1.0 copy-start.2
  213.7 6.1 copy-start.6
  411.4 6.0 copy-start.7
  411.4 6.0 copy-start.14
  411.4 9.5 %slice-start = ((s8[6291456]{0:T(1024)(128)(4,1)}), s8[4194304]{0:T(1024)(128)(4,1)S(1)}, s32[]{:S(2)}) async-start(s8[6291456]{0:T(1024)(128)(4,1)} %bitcast.140), calls=%async_computation.6 | async-start | bytes 8388608
  417.4 3.5 copy-start.17
  417.4 3.5 slice-start.1
  417.4 3.5 copy-start.13
  420.9 4.9 copy-start.19
  425.8 6.5 copy-start.16
  425.8 6.5 copy-start.15
  451.4 106.9 %all-to-all-start.1 = ((bf16[128,12,2048]{2,1,0:T(8,128)(2,1)}), bf16[128,12,2048]{2,1,0:T(8,128)(2,1)}, u32[]{:S(2)}, u32[]{:S(2)}) async-start(bf16[128,12,2048]{2,1,0:T(8,128)(2,1)} %convert_element_type.88), calls=%async_computation.1 | async-start | bytes 16777216 | tf_op jit(solution)/shard_map/all_to_all | solution.py:89
  458.3 166.6 %all-gather.11.cloned.1.call-start = ((), (), s32[]{:S(2)}) async-start(), calls=%async_computation.5 | async-start | bytes 4718592 | tf_op jit(solution)/shard_map/all_gather | solution.py:103
  574.4 4.5 copy-start.9
  578.9 1.2 copy-start.3
  583.1 133.0 %all-reduce.2.cloned.1.call-start = ((), (), s32[]{:S(2)}) async-start(), calls=%async_computation.2 | async-start | bytes 1048576 | tf_op jit(solution)/shard_map/psum | solution.py:109
  583.2 8.9 %copy-start.18 = (f32[1536,512]{1,0:T(8,128)S(1)}, f32[1536,512]{1,0:T(8,128)}, u32[]{:S(2)}) copy-start(f32[1536,512]{1,0:T(8,128)} %copy-done.17) | copy-start | bytes 9437188
  583.2 8.9 %copy-start.20 = (f32[1536,512]{1,0:T(8,128)S(1)}, f32[1536,512]{1,0:T(8,128)}, u32[]{:S(2)}) copy-start(f32[1536,512]{1,0:T(8,128)} %copy-done.19) | copy-start | bytes 9437188
  630.8 8.8 %copy-start.5 = (f32[16,128,128]{2,1,0:T(8,128)S(1)}, f32[16,128,128]{2,1,0:T(8,128)}, u32[]{:S(2)}) copy-start(f32[16,128,128]{2,1,0:T(8,128)} %copy-done.4) | copy-start | bytes 3145732
  639.6 76.6 %copy-start.10 = (bf16[128,2048]{1,0:T(8,128)(2,1)S(1)}, bf16[128,2048]{1,0:T(8,128)(2,1)}, u32[]{:S(2)}) copy-start(bf16[128,2048]{1,0:T(8,128)(2,1)} %param.11) | copy-start | bytes 1572868
  640.8 80.6 %copy-start.1 = (bf16[1,2048,512]{2,1,0:T(8,128)(2,1)S(1)}, bf16[1,2048,512]{2,1,0:T(8,128)(2,1)}, u32[]{:S(2)}) copy-start(bf16[1,2048,512]{2,1,0:T(8,128)(2,1)} %param.15) | copy-start | bytes 6291460
Sparse Core Ops, SparseCore 0:
  10.3 52.1 all-gather.6
  75.6 111.6 all-gather.8
  583.3 41.5 all-gather.10
  630.9 85.2 all-reduce.1
